TPU v7x, 256 devices: a whole 4x4x8 slice. The times are simulated.
256 devices in a mesh: rep: 32 (over y, x, core), tp: 8 (over z).
Axes of the slice: x: 4, y: 4, z: 8, core: 2. Of those that a mesh axis runs over, the one named last changes fastest.
Arguments:
- hidden_in: bfloat16 [256, 5120], P('rep'), may hold values from -40 to 40
- key_cache: bfloat16 [256, 8, 256, 128], P('rep', 'tp'), may hold values from -250 to 250
- value_cache: bfloat16 [256, 8, 256, 128], P('rep', 'tp'), may hold values from -6 to 6
- query_weight: bfloat16 [5120, 3072], P(None, 'tp'), may hold values from -0.078125 to 0.078125
- key_weight: bfloat16 [5120, 1024], P(None, 'tp'), may hold values from -0.078125 to 0.078125
- value_weight: bfloat16 [5120, 1024], P(None, 'tp'), may hold values from -0.078125 to 0.078125
- output_weight: bfloat16 [3072, 5120], P('tp'), may hold values from -0.3125 to 0.3125
- norm_gain: bfloat16 [5120], replicated, may hold values from 0.099609375 to 1.8984375
- countdown_table: bfloat16 [32, 5120], replicated, may hold values from -3 to 3
- countdown_ids: int32 [2, 256], P(None, 'rep'), may hold values from 0 to 31
- lengths: int32 [256], replicated, may hold values from 16 to 254, as said below
- source_slot: int32 [2, 256], replicated, may hold values from 0 to 255, as said below
Outputs:
- hidden_out: bfloat16 [2, 256, 5120], P(None, 'rep')
Inputs may be any that keep to these rules, and one draw needn't show every extreme that they name: `source_slot`: in each step the slots form a permutation; each replica hands exactly 2 rows to other replicas and takes exactly 2, never two from the same replica, into the slots that its leaving rows freed; all other rows keep their slots. In each step there are 2 distinct offsets d, the same for every replica: replica r hands one row to each replica (r + d) mod 32. One offset is 1 in even steps and 32 // 2 in odd steps; the others are drawn. `lengths`: some row holds exactly 254 tokens, some exactly 16.
All inputs are finite; a program needn't handle non-finite values.
Results may differ from a plain program's by a relative error of at most 0.011.
Values may be sent and summed in bfloat16 or wider, within the bound.
A program may use at most 64 MiB of HBM per device.

v0:
```python
import jax
import jax.numpy as jnp
from jax import lax
from jax.sharding import PartitionSpec as P

MOVE = 2
STEPS = 2


THETA = 1000000.0
EPSILON = 1e-06


def rotate(values, positions):
    half_size = values.shape[-1] // 2
    frequency = THETA ** (-jnp.arange(half_size, dtype=jnp.float32) * 2.0 / values.shape[-1])
    angles = positions.astype(jnp.float32)[:, None] * frequency[None, :]
    cosine = jnp.cos(angles)
    sines = jnp.sin(angles)
    cosine = jnp.concatenate([cosine, cosine], -1)[:, None, :]
    sines = jnp.concatenate([sines, sines], -1)[:, None, :]
    front_half = values[..., :half_size]
    back_half = values[..., half_size:]
    turned = jnp.concatenate([-back_half, front_half], -1)
    return values * cosine + turned * sines


def body(
    hidden_in,
    key_cache,
    value_cache,
    query_weight,
    key_weight,
    value_weight,
    output_weight,
    norm_gain,
    countdown_table,
    countdown_ids,
    lengths,
    source_slot,
):
    replicas = lax.axis_size("rep")
    replica_index = lax.axis_index("rep")
    rows_here = hidden_in.shape[0]
    local_heads = key_cache.shape[1]
    capacity = key_cache.shape[2]
    head_size = key_cache.shape[3]
    group_size = query_weight.shape[1] // (local_heads * head_size)
    total_rows = lengths.shape[0]
    first_row = replica_index * rows_here
    everywhere = jnp.arange(total_rows, dtype=jnp.int32)
    positions = jnp.arange(capacity, dtype=jnp.int32)
    token_range = jnp.arange(countdown_table.shape[0], dtype=jnp.int32)
    gain_row = norm_gain.astype(jnp.float32)
    hidden = hidden_in
    cached_keys = key_cache
    cached_values = value_cache
    current = lengths
    results = []
    for step_index in range(STEPS):
        step_source = source_slot[step_index]
        destination = jnp.zeros((total_rows,), jnp.int32).at[step_source].set(everywhere)
        leaving = destination // rows_here != everywhere // rows_here
        my_sources = lax.dynamic_slice_in_dim(step_source, first_row, rows_here)
        source_home = my_sources // rows_here
        arriving = source_home != replica_index
        local_index = jnp.where(arriving, 0, my_sources - first_row)
        kept_keys = jnp.take(cached_keys, local_index, axis=0)
        kept_values = jnp.take(cached_values, local_index, axis=0)
        kept_hidden = jnp.take(hidden, local_index, axis=0)
        leaving_here = lax.dynamic_slice_in_dim(leaving, first_row, rows_here)
        outgoing = jnp.nonzero(leaving_here, size=MOVE, fill_value=0)[0].astype(jnp.int32)
        arrived = (
            lax.all_gather(jnp.take(cached_keys, outgoing, axis=0), "rep", axis=0, tiled=True),
            lax.all_gather(jnp.take(cached_values, outgoing, axis=0), "rep", axis=0, tiled=True),
            lax.all_gather(jnp.take(hidden, outgoing, axis=0), "rep", axis=0, tiled=True),
        )
        outbox_rank = (
            jnp.cumsum(leaving.reshape(replicas, rows_here).astype(jnp.int32), axis=1).reshape(
                total_rows
            )
            - 1
        )
        anchor = source_home * MOVE + jnp.take(outbox_rank, my_sources)
        anchor = jnp.where(arriving, anchor, 0)
        cached_keys = jnp.where(
            arriving[:, None, None, None], jnp.take(arrived[0], anchor, axis=0), kept_keys
        )
        cached_values = jnp.where(
            arriving[:, None, None, None], jnp.take(arrived[1], anchor, axis=0), kept_values
        )
        hidden = jnp.where(arriving[:, None], jnp.take(arrived[2], anchor, axis=0), kept_hidden)
        current = jnp.take(current, step_source)
        here_lengths = lax.dynamic_slice_in_dim(current, first_row, rows_here)
        selector = (countdown_ids[step_index][:, None] == token_range[None, :]).astype(jnp.bfloat16)
        mixture = hidden.astype(jnp.float32) + jnp.dot(
            selector, countdown_table, preferred_element_type=jnp.float32
        )
        inverse_rms = lax.rsqrt(jnp.mean(mixture * mixture, axis=-1, keepdims=True) + EPSILON)
        normed = (mixture * inverse_rms * gain_row).astype(jnp.bfloat16)
        queries = jnp.dot(normed, query_weight, preferred_element_type=jnp.float32).reshape(
            rows_here, local_heads * group_size, head_size
        )
        fresh_key = jnp.dot(normed, key_weight, preferred_element_type=jnp.float32).reshape(
            rows_here, local_heads, head_size
        )
        fresh_value = jnp.dot(normed, value_weight, preferred_element_type=jnp.float32).reshape(
            rows_here, local_heads, head_size
        )
        queries = (
            rotate(queries, here_lengths)
            .astype(jnp.bfloat16)
            .reshape(rows_here, local_heads, group_size, head_size)
        )
        fresh_key = rotate(fresh_key, here_lengths).astype(jnp.bfloat16)
        fresh_value = fresh_value.astype(jnp.bfloat16)
        chosen = (positions[None, :] == here_lengths[:, None])[:, None, :, None]
        cached_keys = jnp.where(chosen, fresh_key[:, :, None, :], cached_keys)
        cached_values = jnp.where(chosen, fresh_value[:, :, None, :], cached_values)
        scores = jnp.einsum(
            "rhgd,rhcd->rhgc", queries, cached_keys, preferred_element_type=jnp.float32
        ) * head_size ** (-0.5)
        allowed = (positions[None, :] <= here_lengths[:, None])[:, None, None, :]
        scores = jnp.where(allowed, scores, -jnp.inf)
        highest = jnp.max(scores, axis=-1, keepdims=True)
        weights = jnp.exp(scores - highest)
        weights = (weights / jnp.sum(weights, axis=-1, keepdims=True)).astype(jnp.bfloat16)
        attended = jnp.einsum(
            "rhgc,rhcd->rhgd", weights, cached_values, preferred_element_type=jnp.float32
        )
        attended = attended.astype(jnp.bfloat16).reshape(
            rows_here, local_heads * group_size * head_size
        )
        partial_value = jnp.dot(attended, output_weight, preferred_element_type=jnp.float32)
        summed = lax.psum(partial_value, "tp")
        hidden = (mixture + summed).astype(jnp.bfloat16)
        results.append(hidden)
        current = current + 1
    return jnp.stack(results)


def solution(mesh):
    placed = (
        P("rep", None),
        P("rep", "tp", None, None),
        P("rep", "tp", None, None),
        P(None, "tp"),
        P(None, "tp"),
        P(None, "tp"),
        P("tp", None),
        P(),
        P(),
        P(None, "rep"),
        P(),
        P(),
    )
    return jax.shard_map(
        body, mesh=mesh, in_specs=placed, out_specs=P(None, "rep", None), check_vma=False
    )
```

profile of v0, /device:TPU:1, one launch (start us, length us, event | category | flops | bytes accessed | tf_op | source)
XLA Modules:
  0.0 397.0 jit_solution(17323820989097896779)
XLA Ops:
  7.4 1.4 scatter_custom_fusion.2
  8.8 1.4 scatter_custom_fusion
  12.7 1.6 gather_fusion.5
  14.4 1.6 gather_fusion.8
  17.8 1.5 gather_fusion
  21.1 1.6 gather_fusion.3
  22.6 1.7 gather_fusion.7
  24.3 1.4 gather_fusion.10
  25.9 26.5 %all-gather = bf16[32,2,5120]{2,1,0:T(2,128)(2,1)S(1)} all-gather(bf16[1,2,5120]{2,1,0:T(2,128)(2,1)S(1)} %fusion.39), channel_id=1, replica_groups=mesh['rep'=32,'tp'=8] {'rep'}, dimensions={0}, use_global_device_ids=true | all-gather | bytes 675840 | tf_op jit(solution)/shard_map/all_gather | solution.py:76
  53.8 1.3 multiply_reduce_fusion.1
  55.2 3.2 convolution_bitcast_fusion.1
  59.4 1.9 gather_fusion.4
  61.4 1.9 gather_fusion.15
  65.2 7.2 %all-gather.7.cloned.1.call-done = bf16[64,1,256,128]{3,2,1,0:T(8,128)(2,1)} async-done(((bf16[2,1,256,128]{3,2,1,0:T(8,128)(2,1)}), bf16[64,1,256,128]{3,2,1,0:T(8,128)(2,1)}) %all-gather.7.cloned.1.call-update) | async-done | bytes 4194320 | tf_op jit(solution)/shard_map/all_gather | solution.py:74
  72.3 3.6 gather_fusion.6
  76.0 49.5 %all-gather.9.cloned.1.call-done = bf16[64,1,256,128]{3,2,1,0:T(8,128)(2,1)} async-done(((bf16[2,1,256,128]{3,2,1,0:T(8,128)(2,1)}), bf16[64,1,256,128]{3,2,1,0:T(8,128)(2,1)}) %all-gather.9.cloned.1.call-update) | async-done | bytes 4194320 | tf_op jit(solution)/shard_map/all_gather | solution.py:75
  125.4 3.6 gather_fusion.9
  129.0 1.6 fusion.23
  132.5 3.4 fusion.56
  140.4 1.4 gather_fusion.18
  141.8 1.4 gather_fusion.21
  143.3 59.4 %all-reduce.3.cloned.1.call-done = f32[8,5120]{1,0:T(8,128)} async-done(((f32[8,5120]{1,0:T(8,128)}), f32[8,5120]{1,0:T(8,128)}) %all-reduce.3.cloned.1.call-update) | async-done | bytes 163856 | tf_op jit(solution)/shard_map/psum | solution.py:135
  204.9 30.2 %all-gather.1 = bf16[32,2,5120]{2,1,0:T(2,128)(2,1)S(1)} all-gather(bf16[1,2,5120]{2,1,0:T(2,128)(2,1)S(1)} %fusion.40), channel_id=1, replica_groups=mesh['rep'=32,'tp'=8] {'rep'}, dimensions={0}, use_global_device_ids=true | all-gather | bytes 675840 | tf_op jit(solution)/shard_map/all_gather | solution.py:76
  236.0 1.3 multiply_reduce_fusion
  237.5 2.7 convolution_bitcast_fusion
  241.0 18.7 %all-gather.11.cloned.1.call-done = bf16[64,1,256,128]{3,2,1,0:T(8,128)(2,1)} async-done(((bf16[2,1,256,128]{3,2,1,0:T(8,128)(2,1)}), bf16[64,1,256,128]{3,2,1,0:T(8,128)(2,1)}) %all-gather.11.cloned.1.call-update) | async-done | bytes 4194320 | tf_op jit(solution)/shard_map/all_gather | solution.py:74
  259.7 2.8 gather_fusion.17
  262.5 50.4 %all-gather.13.cloned.1.call-done = bf16[64,1,256,128]{3,2,1,0:T(8,128)(2,1)} async-done(((bf16[2,1,256,128]{3,2,1,0:T(8,128)(2,1)}), bf16[64,1,256,128]{3,2,1,0:T(8,128)(2,1)}) %all-gather.13.cloned.1.call-update) | async-done | bytes 4194320 | tf_op jit(solution)/shard_map/all_gather | solution.py:75
  313.0 2.8 gather_fusion.20
  315.9 1.7 fusion.101
  318.3 3.4 fusion.53
  321.7 66.8 %all-reduce.5.cloned.1.call-done = f32[8,5120]{1,0:T(8,128)} async-done(((f32[8,5120]{1,0:T(8,128)}), f32[8,5120]{1,0:T(8,128)}) %all-reduce.5.cloned.1.call-update) | async-done | bytes 163856 | tf_op jit(solution)/shard_map/psum | solution.py:135
  (129 shorter events, 23.8 us)
Async XLA Ops:
  6.5 57.7 %copy-start = (bf16[5120,128]{1,0:T(8,128)(2,1)S(1)}, bf16[5120,128]{1,0:T(8,128)(2,1)}, u32[]{:S(2)}) copy-start(bf16[5120,128]{1,0:T(8,128)(2,1)} %param.32) | copy-start | bytes 3932164
  6.5 17.8 %copy-start.4 = (bf16[8,1,256,128]{3,2,1,0:T(8,128)(2,1)S(1)}, bf16[8,1,256,128]{3,2,1,0:T(8,128)(2,1)}, u32[]{:S(2)}) copy-start(bf16[8,1,256,128]{3,2,1,0:T(8,128)(2,1)} %param.30) | copy-start | bytes 1572868
  6.5 46.1 %copy-start.6 = (bf16[5120]{0:T(1024)(128)(2,1)S(1)}, bf16[5120]{0:T(1024)(128)(2,1)}, u32[]{:S(2)}) copy-start(bf16[5120]{0:T(1024)(128)(2,1)} %param.35) | copy-start | bytes 30724
  6.5 65.8 %all-gather.7.cloned.1.call-start = ((), (), s32[]{:S(2)}) async-start(), calls=%async_computation | async-start | bytes 4325376 | tf_op jit(solution)/shard_map/all_gather | solution.py:74
  8.8 44.5 %copy-start.13 = (s32[2,8]{1,0:T(2,128)S(1)}, s32[2,8]{1,0:T(2,128)}, u32[]{:S(2)}) copy-start(s32[2,8]{1,0:T(2,128)} %param.37) | copy-start | bytes 196
  16.8 108.6 %all-gather.9.cloned.1.call-start = ((), (), s32[]{:S(2)}) async-start(), calls=%async_computation.1 | async-start | bytes 4325376 | tf_op jit(solution)/shard_map/all_gather | solution.py:75
  17.5 185.2 %all-reduce.3.cloned.1.call-start = ((), (), s32[]{:S(2)}) async-start(), calls=%async_computation.2 | async-start | bytes 327680 | tf_op jit(solution)/shard_map/psum | solution.py:135
  25.8 33.6 %copy-start.1 = (s32[256]{0:T(256)S(1)}, s32[256]{0:T(256)}, u32[]{:S(2)}) copy-start(s32[256]{0:T(256)} %param.38) | copy-start | bytes 3076
  55.2 9.7 %copy-start.2 = (bf16[5120,128]{1,0:T(8,128)(2,1)S(1)}, bf16[5120,128]{1,0:T(8,128)(2,1)}, u32[]{:S(2)}) copy-start(bf16[5120,128]{1,0:T(8,128)(2,1)} %param.33) | copy-start | bytes 3932164
  135.9 123.7 %all-gather.11.cloned.1.call-start = ((), (), s32[]{:S(2)}) async-start(), calls=%async_computation.3 | async-start | bytes 4325376 | tf_op jit(solution)/shard_map/all_gather | solution.py:74
  136.8 176.2 %all-gather.13.cloned.1.call-start = ((), (), s32[]{:S(2)}) async-start(), calls=%async_computation.4 | async-start | bytes 4325376 | tf_op jit(solution)/shard_map/all_gather | solution.py:75
  137.4 251.1 %all-reduce.5.cloned.1.call-start = ((), (), s32[]{:S(2)}) async-start(), calls=%async_computation.5 | async-start | bytes 327680 | tf_op jit(solution)/shard_map/psum | solution.py:135
  139.1 96.1 %copy-start.7 = (pred[8]{0:T(512)(128)(4,1)}, pred[8]{0:T(512)(128)(4,1)S(1)}, u32[]{:S(2)}) copy-start(pred[8]{0:T(512)(128)(4,1)S(1)} %get-tuple-element.18) | copy-start | bytes 28
  235.4 5.4 %copy-start.3 = (bf16[5120,128]{1,0:T(8,128)(2,1)S(1)}, bf16[5120,128]{1,0:T(8,128)(2,1)}, u32[]{:S(2)}) copy-start(bf16[5120,128]{1,0:T(8,128)(2,1)} %param.33) | copy-start | bytes 3932164
  237.4 78.4 %copy-start.8 = (pred[8]{0:T(512)(128)(4,1)S(1)}, pred[8]{0:T(512)(128)(4,1)}, u32[]{:S(2)}) copy-start(pred[8]{0:T(512)(128)(4,1)} %copy-done.7) | copy-start | bytes 28
  237.4 78.4 %copy-start.9 = (pred[8,256]{1,0:T(8,128)(4,1)S(1)}, pred[8,256]{1,0:T(8,128)(4,1)}, u32[]{:S(2)}) copy-start(pred[8,256]{1,0:T(8,128)(4,1)} %get-tuple-element.68) | copy-start | bytes 6148
  237.4 78.4 %copy-start.10 = (pred[8,256]{1,0:T(8,128)(4,1)S(1)}, pred[8,256]{1,0:T(8,128)(4,1)}, u32[]{:S(2)}) copy-start(pred[8,256]{1,0:T(8,128)(4,1)} %get-tuple-element.67) | copy-start | bytes 6148
  237.5 78.4 %copy-start.11 = (pred[8]{0:T(512)(128)(4,1)S(1)}, pred[8]{0:T(512)(128)(4,1)}, u32[]{:S(2)}) copy-start(pred[8]{0:T(512)(128)(4,1)} %get-tuple-element.14) | copy-start | bytes 28
  237.5 78.4 %copy-start.12 = (pred[8]{0:T(512)(128)(4,1)S(1)}, pred[8]{0:T(512)(128)(4,1)}, u32[]{:S(2)}) copy-start(pred[8]{0:T(512)(128)(4,1)} %get-tuple-element.20) | copy-start | bytes 28
  240.2 77.4 %copy-start.5 = (bf16[8,256,128]{2,1,0:T(8,128)(2,1)S(1)}, bf16[8,256,128]{2,1,0:T(8,128)(2,1)}, u32[]{:S(2)}) copy-start(bf16[8,256,128]{2,1,0:T(8,128)(2,1)} %gather_fusion.21) | copy-start | bytes 1572868
Sparse Core Ops, SparseCore 0:
  16.9 55.3 all-gather.6
  74.9 50.5 all-gather.8
  136.1 66.6 all-reduce.2
  205.5 54.1 all-gather.10
  262.4 50.5 all-gather.12
  321.8 66.6 all-reduce.4
where the time goes:
time: 402 us; the launch traced here: 397 us
  waiting for transfers between devices  253 us (63%)
  blocking collectives  56.7 us (14%)
  local copies, waits for them, and re-layouts  38.9 us (10%)
  matrix products  19.6 us (5%)
  other arithmetic  14.3 us (4%)
  between operations  14 us (3%)
    psum x2, waiting for transfers between devices, body(): summed = lax.psum(partial_value, 'tp')  126 us
    all_gather x2, waiting for transfers between devices, body(): lax.all_gather(jnp.take(cached_values, outgoing, axis=0), 'rep', axis=0,...  99.9 us
    all_gather x2, blocking collectives, body(): lax.all_gather(jnp.take(hidden, outgoing, axis=0), 'rep', axis=0, tiled=T...  56.7 us
    all_gather x2, waiting for transfers between devices, body(): lax.all_gather(jnp.take(cached_keys, outgoing, axis=0), 'rep', axis=0, ti...  25.8 us
  transfers between devices with their start and end apart: 6, of which 6 were waited for; matrix products, arithmetic and copies ran while one was open for 11% of the time, Pallas kernels for 0%

commit v1 on v0

v1 whole, which is shorter than its diff:
```python
import functools
import math

import jax
import jax.numpy as jnp
from jax import lax
from jax.experimental import pallas as pl
from jax.experimental.pallas import tpu as pltpu
from jax.sharding import PartitionSpec as P

MESH = pl.DeviceIdType.MESH
F32 = jnp.float32
BF16 = jnp.bfloat16
THETA = 1000000.0
EPSILON = 1e-06
LANES = 128
MOVE = 2
KEEP = 4


def iota(shape, dim):
    return lax.broadcasted_iota(jnp.int32, shape, dim)


def ones_at(mask):
    return jnp.where(mask, 1.0, 0.0).astype(F32)


def lane_pick(index, row):
    lanes = iota((index.shape[0], row.shape[1]), 1)
    return jnp.sum(jnp.where(lanes == index, row, 0.0), axis=1, keepdims=True).astype(jnp.int32)


def pack(x):
    rows, width = x.shape
    high = (width // LANES + 1) // 2 * LANES
    low = jnp.concatenate([x[:, high:], jnp.zeros((rows, 2 * high - width), x.dtype)], axis=1)
    return jnp.concatenate([x[:, :high], low], axis=0).astype(BF16)


def unpack(y, width):
    y = y.astype(F32)
    rows, high = y.shape[0] // 2, y.shape[1]
    return jnp.concatenate([y[:rows], y[rows:, : width - high]], axis=1)


def stack_groups(x):
    return jnp.concatenate(
        [x[:, c : c + LANES] for c in range(0, x.shape[1], LANES)], axis=0
    )


def spread_groups(x, rows):
    return jnp.concatenate([x[c : c + rows] for c in range(0, x.shape[0], rows)], axis=1)


def dot(a, b):
    return jnp.dot(a, b, preferred_element_type=F32)


def kernel(
    reps,
    tps,
    hid_hbm,
    keys_hbm,
    values_hbm,
    wq_hbm,
    wk_hbm,
    wv_hbm,
    wo_hbm,
    gain_hbm,
    table_hbm,
    ids_hbm,
    len_hbm,
    src_hbm,
    out_hbm,
    hid_v,
    keys_v,
    values_v,
    wqkv_v,
    wo_v,
    gain_v,
    table_v,
    ids_v,
    len_s,
    src_v,
    gains_v,
    wide_v,
    sums_v,
    tab_v,
    rank_v,
    first_v,
    last_v,
    id_send,
    id_recv,
    part_send,
    part_recv,
    home_buf,
    first_buf,
    last_buf,
    row_send,
    row_recv,
    att_send,
    att_recv,
    load_sem,
    weight_sem,
    out_w_sem,
    id_ssem,
    id_rsem,
    part_ssem,
    part_rsem,
    gath_ssem,
    gath_rsem,
    row_ssem,
    row_rsem,
    att_ssem,
    att_rsem,
    out_sem,
):
    r = lax.axis_index("rep")
    t = lax.axis_index("tp")
    rows = hid_v.shape[0]
    chunk = wo_v.shape[2]
    groups = chunk // LANES
    heads = wo_v.shape[1] // LANES
    qcols = heads * LANES
    total_rows = rows * reps
    capacity = keys_v.shape[1]
    tokens = table_v.shape[1]
    model = chunk * tps
    half = LANES // 2
    erows = row_send.shape[0]
    arows = att_send.shape[0]

    def chunk_cols(c):
        return pl.ds(pl.multiple_of(c * chunk, LANES), chunk)

    def chunk_rows(c):
        return pl.ds(pl.multiple_of(c * chunk, LANES), chunk)

    small = [
        pltpu.make_async_copy(src_hbm, src_v, load_sem.at[0]),
        pltpu.make_async_copy(ids_hbm, ids_v, load_sem.at[1]),
        pltpu.make_async_copy(len_hbm, len_s, load_sem.at[2]),
        pltpu.make_async_copy(hid_hbm, hid_v, load_sem.at[3]),
        pltpu.make_async_copy(gain_hbm, gain_v, load_sem.at[4]),
    ]
    for copy in small:
        copy.start()

    def table_copy(c):
        return pltpu.make_async_copy(
            table_hbm.at[:, chunk_cols(c)], table_v.at[c], load_sem.at[7 + c]
        )

    for c in range(tps):
        table_copy(c).start()

    def weight_copies(c):
        return [
            pltpu.make_async_copy(
                wq_hbm.at[chunk_rows(c), :], wqkv_v.at[c, :, pl.ds(0, qcols)], weight_sem.at[0, c]
            ),
            pltpu.make_async_copy(
                wk_hbm.at[chunk_rows(c), :], wqkv_v.at[c, :, pl.ds(qcols, LANES)], weight_sem.at[1, c]
            ),
            pltpu.make_async_copy(
                wv_hbm.at[chunk_rows(c), :],
                wqkv_v.at[c, :, pl.ds(qcols + LANES, LANES)],
                weight_sem.at[2, c],
            ),
        ]

    @pl.loop(0, tps)
    def _(c):
        for copy in weight_copies(c):
            copy.start()

    cache_copies = [
        pltpu.make_async_copy(keys_hbm, keys_v, load_sem.at[5]),
        pltpu.make_async_copy(values_hbm, values_v, load_sem.at[6]),
    ]
    for copy in cache_copies:
        copy.start()

    def out_weight_copy(c):
        return pltpu.make_async_copy(wo_hbm.at[:, chunk_cols(c)], wo_v.at[c], out_w_sem.at[c])

    @pl.loop(0, tps)
    def _(c):
        out_weight_copy(c).start()

    barrier = pltpu.get_barrier_semaphore()

    @pl.loop(1, reps)
    def _(d):
        pl.semaphore_signal(
            barrier, inc=1, device_id=(lax.rem(r + d, reps), t), device_id_type=MESH
        )

    @pl.loop(1, tps)
    def _(d):
        pl.semaphore_signal(
            barrier, inc=1, device_id=(r, lax.rem(t + d, tps)), device_id_type=MESH
        )

    small[1].wait()
    id_send[...] = jnp.zeros_like(id_send)
    id_send[:, 0:rows] = ids_v[...]
    pl.semaphore_wait(barrier, reps + tps - 2)

    def to_all_reps(src, dst, send_sem, recv_sem):
        @pl.loop(1, reps)
        def _(d):
            pltpu.make_async_remote_copy(
                src_ref=src,
                dst_ref=dst.at[r],
                send_sem=send_sem,
                recv_sem=recv_sem,
                device_id=(lax.rem(r + d, reps), t),
                device_id_type=MESH,
            ).start()

    def wait_reps(dst, sem):
        blocks = dst.at[pl.ds(0, reps - 1)]
        pltpu.make_async_copy(blocks, blocks, sem).wait()

    to_all_reps(id_send, id_recv, id_ssem, id_rsem)
    id_recv[r] = id_send[...]

    small[0].wait()
    src0 = src_v[0:1, :].astype(F32)
    src1 = src_v[1:2, :].astype(F32)
    square = (total_rows, total_rows)
    subs, lanes = iota(square, 0), iota(square, 1)
    far = (subs >> 3) != (lanes >> 3)
    subs_f = subs.astype(F32)
    slot0 = ones_at(src0 == subs_f)
    slot1 = ones_at(src1 == subs_f)
    both = dot(slot0.astype(BF16), slot1.astype(BF16))
    leaves = jnp.where(far, slot0 + both, 0.0).astype(BF16)
    moved = ones_at(dot(leaves, jnp.ones((total_rows, LANES), BF16)) > 0.5)
    before = ones_at(((subs >> 3) == (lanes >> 3)) & (lanes < subs)).astype(BF16)
    rank = dot(before, moved.astype(BF16))
    rank_v[...] = jnp.where(moved > 0.5, rank, float(rows))

    row_of = iota((rows, total_rows), 0) + r * rows
    glanes = iota((rows, total_rows), 1)
    glanes_f = glanes.astype(F32)
    to0 = jnp.sum(jnp.where(src0 == row_of.astype(F32), glanes_f, 0.0), axis=1, keepdims=True)
    to1 = jnp.sum(jnp.where(src1 == to0, glanes_f, 0.0), axis=1, keepdims=True)
    to0, to1 = to0.astype(jnp.int32), to1.astype(jnp.int32)

    own_rank = rank_v[pl.ds(pl.multiple_of(r * rows, rows), rows), :]
    diagonal = iota((rows, LANES), 0) == (iota((rows, LANES), 1) & (rows - 1))
    rank_lane = jnp.sum(jnp.where(diagonal, own_rank, 0.0), axis=0, keepdims=True)

    def gather_sent(sent, kinds):
        shape = (sent, kinds * rows)
        p, q = iota(shape, 0), iota(shape, 1)
        want = (p & (KEEP - 1)).astype(F32)
        hit = ((p >> 2) == (q >> 3)) & (rank_lane[:, : kinds * rows] == want)
        return ones_at(hit).astype(BF16)

    row_pick = gather_sent(erows, groups)
    att_pick = gather_sent(arows, heads)

    def take_slots(kinds, sent, final):
        count = kinds * rows
        slot = r * rows + (iota((count, 1), 0) & (rows - 1))
        if final:
            slot = lane_pick(slot, src1)
        row = lane_pick(slot, src0)
        kind = iota((count, 1), 0) >> 3
        home = row >> 3
        one = ones_at(iota((count, total_rows), 1) == row).astype(BF16)
        k = dot(one, rank_v[...].astype(BF16)).astype(jnp.int32)[:, 0:1]
        far_at = jnp.where(home == r, -1, home * sent + kind * KEEP + k)
        near_at = jnp.where(home == r, kind * rows + (row & (rows - 1)), -1)
        from_far = ones_at(iota((count, reps * sent), 1) == far_at).astype(BF16)
        from_near = ones_at(iota((count, count), 1) == near_at).astype(BF16)
        return from_far, from_near

    first_far, first_near = take_slots(groups, erows, False)
    last_far, last_near = take_slots(groups, erows, True)
    att_far, att_near = take_slots(heads, arows, True)

    small[2].wait()
    sub8 = iota((rows, 1), 0)
    position = jnp.zeros((rows, 1), jnp.int32)
    for i in range(rows):
        position = jnp.where(sub8 == i, len_s[r * rows + i], position)
    lane128 = iota((1, LANES), 1)
    exponent = (lane128 & (half - 1)).astype(F32) * (-2.0 / LANES)
    frequency = jnp.exp(exponent * math.log(THETA))
    sign = jnp.where(lane128 < half, -1.0, 1.0)

    def turns(place):
        angles = place.astype(F32) * frequency
        return jnp.cos(angles), jnp.sin(angles) * sign

    token_lane = iota((rows, tokens), 1)

    def token_pick(ids):
        return ones_at(token_lane == ids)

    def hidden_chunk(c):
        return hid_v[:, chunk_cols(c)].astype(F32)

    lane8 = iota((rows, LANES), 1)

    def local_pick(step, slot):
        mine = jnp.where(lane8 == slot, id_send[step : step + 1, :].astype(F32), 0.0)
        return token_pick(jnp.sum(mine, axis=1, keepdims=True).astype(jnp.int32))

    stay_pick = local_pick(0, to0 & (rows - 1)).astype(BF16)
    slot_pick = local_pick(1, sub8)
    leaves0 = ones_at((to0 >> 3) != r)
    earlier = ones_at(iota((rows, rows), 1) < iota((rows, rows), 0)).astype(BF16)
    order = dot(earlier, jnp.broadcast_to(leaves0, (rows, LANES)).astype(BF16))[:, 0:1]
    movers = [(leaves0 > 0.5) & (order == float(k)) for k in range(MOVE)]
    for copy in small[3:]:
        copy.wait()
    gain = gain_v[...].astype(F32).reshape(1, model)
    for c in range(tps):
        table_copy(c).wait()
        gains_v[c] = jnp.broadcast_to(gain[:, c * chunk : (c + 1) * chunk], (rows, chunk))

    def gain_chunk(c):
        return gains_v[c, 0:1, :]

    def squares_of(mixture):
        sq = mixture * mixture
        return sum(sq[:, g * LANES : (g + 1) * LANES] for g in range(groups))

    def project(c, mixture, carry):
        acc, squares = carry
        scaled = (mixture * gain_chunk(c)).astype(BF16)
        return acc + dot(scaled, wqkv_v[c]), squares + squares_of(mixture)

    def normalise(carry):
        acc, squares = carry
        mean = jnp.sum(squares, axis=1, keepdims=True) * (1.0 / model)
        return acc * lax.rsqrt(mean + EPSILON)

    zero_carry = (jnp.zeros((rows, qcols + 2 * LANES), F32), jnp.zeros((rows, LANES), F32))
    cap_lane = iota((rows, capacity), 1)
    scale = LANES**-0.5

    def round16(x):
        return x.astype(BF16).astype(F32)

    def attend(qkv, place, fresh):
        cosine, sine = turns(place)

        def rotate(x):
            return round16(x * cosine + pltpu.roll(x, half, 1) * sine)

        queries = [rotate(qkv[:, h * LANES : (h + 1) * LANES]) for h in range(heads)]
        fresh_key = rotate(qkv[:, qcols : qcols + LANES])
        fresh_value = round16(qkv[:, qcols + LANES :])
        fresh = fresh + [(fresh_key, fresh_value, place)]
        stacked = jnp.concatenate(queries, axis=0).astype(BF16)
        scores = [jnp.zeros((rows, capacity), F32)] * heads
        for i in range(rows):
            one = lax.dot_general(
                stacked, keys_v[i], (((1,), (1,)), ((), ())), preferred_element_type=F32
            )
            for h in range(heads):
                scores[h] = jnp.where(sub8 == i, one[h * rows : (h + 1) * rows], scores[h])
        weights, extra = [], []
        for h in range(heads):
            s = scores[h] * scale
            news = [jnp.sum(queries[h] * k, axis=1, keepdims=True) * scale for k, _, _ in fresh]
            for new, (_, _, at) in zip(news, fresh):
                s = jnp.where(cap_lane == at, new, s)
            s = jnp.where(cap_lane <= place, s, -jnp.inf)
            top = jnp.max(s, axis=1, keepdims=True)
            e = jnp.exp(s - top)
            total = jnp.sum(e, axis=1, keepdims=True)
            w = e / total
            for _, _, at in fresh:
                w = jnp.where(cap_lane == at, 0.0, w)
            weights.append(w)
            extra.append([round16(jnp.exp(new - top) / total) for new in news])
        stacked = jnp.concatenate(weights, axis=0).astype(BF16)
        outs = [jnp.zeros((rows, LANES), F32)] * heads
        for i in range(rows):
            one = dot(stacked, values_v[i])
            for h in range(heads):
                outs[h] = jnp.where(sub8 == i, one[h * rows : (h + 1) * rows], outs[h])
        for h in range(heads):
            for w, (_, v, _) in zip(extra[h], fresh):
                outs[h] = outs[h] + w * v
        return jnp.concatenate(outs, axis=0).astype(BF16), fresh

    def part_copy(step, to, src):
        return pltpu.make_async_remote_copy(
            src_ref=part_send.at[step, to],
            dst_ref=part_recv.at[step, src],
            send_sem=part_ssem.at[step, to],
            recv_sem=part_rsem.at[step, src],
            device_id=(r, to),
            device_id_type=MESH,
        )

    def far_first(n):
        odd = lax.rem(n, 2)
        return tps // 2 + (lax.div(n, 2) + odd) * (1 - 2 * odd)

    def output_sum(step, attended, wait_weights, meanwhile):
        @pl.loop(0, tps - 1)
        def _(n):
            to = lax.rem(t + far_first(n), tps)
            if wait_weights:
                out_weight_copy(to).wait()
            part_send[step, to] = pack(dot(attended, wo_v[to]))
            part_copy(step, to, t).start()

        if wait_weights:
            out_weight_copy(t).wait()
        total = dot(attended, wo_v[t])
        meanwhile()

        def add(d, total):
            src = lax.rem(t + d, tps)
            part_copy(step, t, src).wait_recv()
            return total + unpack(part_recv[step, src], chunk)

        return lax.fori_loop(1, tps, add, total)

    def gather_copy(which, buf, to, src):
        return pltpu.make_async_remote_copy(
            src_ref=buf.at[src],
            dst_ref=buf.at[src],
            send_sem=gath_ssem.at[which, to],
            recv_sem=gath_rsem.at[which, src],
            device_id=(r, to),
            device_id_type=MESH,
        )

    def gather_start(which, buf, block):
        buf[t] = block

        @pl.loop(0, tps - 1)
        def _(n):
            gather_copy(which, buf, lax.rem(t + far_first(n), tps), t).start()

    sums_v[...] = jnp.zeros_like(sums_v)
    wide_v[...] = jnp.zeros_like(wide_v)

    @pl.loop(0, tps)
    def _(c):
        for copy in weight_copies(c):
            copy.wait()
        hid = hidden_chunk(c)
        table = table_v[c]
        blocks = [hid + dot(stay_pick, table)]
        for mover in movers:
            row = jnp.sum(jnp.where(mover, hid, 0.0), axis=0, keepdims=True)
            blocks.append(row + table.astype(F32))
        mixture = jnp.concatenate(blocks, axis=0)
        wide_v[...] += dot((mixture * gain_chunk(c)).astype(BF16), wqkv_v[c])
        sums_v[...] += squares_of(mixture)

    wait_reps(id_recv, id_rsem)
    id_rows = [jnp.zeros((rows, LANES), F32), jnp.zeros((rows, LANES), F32)]
    for h in range(reps):
        block = id_recv[h].astype(F32)
        for step, slot in enumerate((to0, to1)):
            id_rows[step] = jnp.where((slot >> 3) == h, block[step : step + 1, :], id_rows[step])
    ids = []
    for step, slot in enumerate((to0, to1)):
        mine = jnp.where(lane8 == (slot & (rows - 1)), id_rows[step], 0.0)
        ids.append(jnp.sum(mine, axis=1, keepdims=True))
    now_pick, next_pick = [token_pick(i.astype(jnp.int32)) for i in ids]
    carry = wide_v[0:rows, :], sums_v[0:rows, :]
    token_sub = iota((tokens, 1), 0).astype(F32)
    for k, mover in enumerate(movers):
        token = jnp.sum(jnp.where(mover, ids[0], 0.0), axis=0, keepdims=True)
        at = slice(rows + k * tokens, rows + (k + 1) * tokens)
        carry = tuple(
            jnp.where(
                mover,
                jnp.sum(jnp.where(token_sub == token, wide[at, :], 0.0), axis=0, keepdims=True),
                kept,
            )
            for wide, kept in zip((wide_v, sums_v), carry)
        )
    qkv = normalise(carry)
    for copy in cache_copies:
        copy.wait()
    attended, fresh = attend(qkv, position, [])
    attended = spread_groups(attended, rows)

    def find_tokens():
        picks = jnp.concatenate([next_pick, slot_pick], axis=0).astype(BF16)
        for c in range(tps):
            tab_v[c] = dot(picks, table_v[c])
        mix.append(hidden_chunk(t) + dot(now_pick.astype(BF16), table_v[t]))

    mix = []
    summed = output_sum(0, attended, True, find_tokens)
    hidden = round16(mix[0] + summed)
    gather_start(0, home_buf, pack(hidden))
    own_groups = stack_groups(hidden).astype(BF16)
    row_send[...] = dot(row_pick, own_groups).astype(BF16)
    to_all_reps(row_send, row_recv, row_ssem, row_rsem)
    row_recv[r] = row_send[...]

    carry = project(t, hidden + tab_v[t, 0:rows], zero_carry)

    def next_project(n, carry):
        src = lax.rem(t + far_first(tps - 2 - n), tps)
        gather_copy(0, home_buf, t, src).wait_recv()
        return project(src, unpack(home_buf[src], chunk) + tab_v[src, 0:rows], carry)

    qkv = normalise(lax.fori_loop(0, tps - 1, next_project, carry))

    attended, _ = attend(qkv, position + 1, fresh)
    att_send[...] = dot(att_pick, attended).astype(BF16)
    to_all_reps(att_send, att_recv, att_ssem, att_rsem)
    att_recv[r] = att_send[...]

    wait_reps(row_recv, row_rsem)
    received = row_recv[...].reshape(reps * erows, LANES)
    first = spread_groups(dot(first_far, received) + dot(first_near, own_groups), rows)
    last = spread_groups(dot(last_far, received) + dot(last_near, own_groups), rows)
    last = last + tab_v[t, rows:]
    gather_start(1, first_buf, pack(first))

    wait_reps(att_recv, att_rsem)
    received = att_recv[...].reshape(reps * arows, LANES)
    attended = (dot(att_far, received) + dot(att_near, attended)).astype(BF16)
    attended = spread_groups(attended, rows)

    def result(which, buf, out_v):
        @pl.loop(1, tps)
        def _(d):
            gather_copy(which, buf, t, lax.rem(t + d, tps)).wait_recv()

        for c in range(tps):
            cols = slice(c * chunk, (c + 1) * chunk)
            out_v[:, cols] = unpack(buf[c], chunk).astype(BF16)
        copy = pltpu.make_async_copy(out_v, out_hbm.at[which - 1], out_sem.at[which - 1])
        copy.start()
        return copy

    outs = []
    summed = output_sum(1, attended, False, lambda: outs.append(result(1, first_buf, first_v)))
    hidden = last + summed
    gather_start(2, last_buf, pack(hidden))
    outs.append(result(2, last_buf, last_v))

    wait_reps(id_recv, id_ssem)
    wait_reps(row_recv, row_ssem)
    wait_reps(att_recv, att_ssem)

    @pl.loop(1, tps)
    def _(d):
        to = lax.rem(t + d, tps)
        for step in range(2):
            part_copy(step, to, t).wait_send()
        for which, buf in enumerate((home_buf, first_buf, last_buf)):
            gather_copy(which, buf, to, t).wait_send()

    for copy in outs:
        copy.wait()


def body(
    reps,
    tps,
    hidden_in,
    key_cache,
    value_cache,
    query_weight,
    key_weight,
    value_weight,
    output_weight,
    norm_gain,
    countdown_table,
    countdown_ids,
    lengths,
    source_slot,
):
    rows, model = hidden_in.shape
    capacity, head = key_cache.shape[2:]
    chunk = model // tps
    qcols = query_weight.shape[1]
    heads = qcols // head
    tokens = countdown_table.shape[0]
    steps = countdown_ids.shape[0]
    total_rows = lengths.shape[0]
    groups = chunk // LANES
    high = (groups + 1) // 2 * LANES
    erows = -(-groups * KEEP // 16) * 16
    arows = -(-heads * KEEP // 16) * 16
    block = (2 * rows, high)
    dma, vmem = pltpu.SemaphoreType.DMA, pltpu.VMEM
    scratch = [
        vmem((rows, model), BF16),
        vmem((rows, capacity, head), BF16),
        vmem((rows, capacity, head), BF16),
        vmem((tps, chunk, qcols + 2 * head), BF16),
        vmem((tps, qcols, chunk), BF16),
        vmem((model,), BF16),
        vmem((tps, tokens, chunk), BF16),
        vmem((steps, rows), jnp.int32),
        pltpu.SMEM((total_rows,), jnp.int32),
        vmem((steps, total_rows), jnp.int32),
        vmem((tps, rows, chunk), F32),
        vmem((rows + MOVE * tokens, qcols + 2 * head), F32),
        vmem((rows + MOVE * tokens, LANES), F32),
        vmem((tps, 2 * rows, chunk), F32),
        vmem((total_rows, LANES), F32),
        vmem((rows, model), BF16),
        vmem((rows, model), BF16),
        vmem((steps, LANES), jnp.int32),
        vmem((reps, steps, LANES), jnp.int32),
        vmem((steps, tps) + block, BF16),
        vmem((steps, tps) + block, BF16),
        vmem((tps,) + block, BF16),
        vmem((tps,) + block, BF16),
        vmem((tps,) + block, BF16),
        vmem((erows, LANES), BF16),
        vmem((reps, erows, LANES), BF16),
        vmem((arows, LANES), BF16),
        vmem((reps, arows, LANES), BF16),
        dma((7 + tps,)),
        dma((3, tps)),
        dma((tps,)),
        dma,
        dma,
        dma((steps, tps)),
        dma((steps, tps)),
        dma((3, tps)),
        dma((3, tps)),
        dma,
        dma,
        dma,
        dma,
        dma((2,)),
    ]
    return pl.pallas_call(
        functools.partial(kernel, reps, tps),
        out_shape=jax.ShapeDtypeStruct((steps, rows, model), BF16),
        in_specs=[pl.BlockSpec(memory_space=pl.ANY)] * 12,
        out_specs=pl.BlockSpec(memory_space=pl.ANY),
        scratch_shapes=scratch,
        compiler_params=pltpu.CompilerParams(
            collective_id=0, has_side_effects=True, vmem_limit_bytes=60 * 2**20
        ),
    )(
        hidden_in,
        key_cache.reshape(rows, capacity, head),
        value_cache.reshape(rows, capacity, head),
        query_weight,
        key_weight,
        value_weight,
        output_weight,
        norm_gain,
        countdown_table,
        countdown_ids,
        lengths,
        source_slot,
    )


def solution(mesh):
    placed = (
        P("rep", None),
        P("rep", "tp", None, None),
        P("rep", "tp", None, None),
        P(None, "tp"),
        P(None, "tp"),
        P(None, "tp"),
        P("tp", None),
        P(),
        P(),
        P(None, "rep"),
        P(),
        P(),
    )
    return jax.shard_map(
        functools.partial(body, mesh.shape["rep"], mesh.shape["tp"]),
        mesh=mesh,
        in_specs=placed,
        out_specs=P(None, "rep", None),
        check_vma=False,
    )
```

time: 402 us -> 45.8 us (0.11); the launches traced: 397 us -> 45.7 us
  waiting for transfers between devices: 253 us -> 0 us
  blocking collectives: 56.7 us -> 0 us
  Pallas kernels: 0 us -> 44.1 us
  local copies, waits for them, and re-layouts: 38.9 us -> 1.59 us
  matrix products: 19.6 us -> 0 us
  other arithmetic: 14.3 us -> 0 us
  between operations: 14 us -> 0.01 us
    psum x2 -> x0, waiting for transfers between devices: 126 us -> none  [body(): summed = lax.psum(partial_value, 'tp')]
    all_gather x4 -> x0, waiting for transfers between devices: 126 us -> none  [the longest x2 99.9 us: body(): lax.all_gather(jnp.take(cached_values, outgoing, axis=0), 'rep', axis=0,...]
    all_gather x2 -> x0, blocking collectives: 56.7 us -> none  [body(): lax.all_gather(jnp.take(hidden, outgoing, axis=0), 'rep', axis=0, tiled=T...]
    pallas_call x0 -> x1, Pallas kernels: none -> 44.1 us  [body(): pl.pallas_call(functools.partial(kernel, reps, tps), out_shape=jax.ShapeD...]
    gather x22 -> x0, local copies, waits for them, and re-layouts: 33.9 us -> none  [the longest x2 6.47 us: body(): jnp.take(arrived[0], anchor, axis=0)]
    dot_general x12 -> x0, matrix products: 17.4 us -> none  [the longest x2 6.83 us: body(): jnp.dot(attended, output_weight, preferred_element_type=jnp.float32)]
    another operation x9 -> x0, other arithmetic: 4.25 us -> none
  transfers between devices with their start and end apart: 6 -> 0, of which waited for: 6 -> 0; matrix products, arithmetic and copies ran while one was open for 11% -> 0% of each run, Pallas kernels for 0% -> 0%
where the time goes in v1:
time: 45.8 us; the launch traced here: 45.7 us
  Pallas kernels  44.1 us (96%)
  local copies, waits for them, and re-layouts  1.59 us (3%)
    pallas_call x1, Pallas kernels, body(): pl.pallas_call(functools.partial(kernel, reps, tps), out_shape=jax.ShapeD...  44.1 us
    unnamed x1, local copies, waits for them, and re-layouts  1.59 us

profile of v1, /device:TPU:1, one launch (start us, length us, event | category | flops | bytes accessed | tf_op | source)
XLA Modules:
  0.0 45.7 jit_solution(5047755347881042787)
XLA Ops:
  0.0 44.1 %shard_map.118 = bf16[2,8,5120]{2,1,0:T(8,128)(2,1)} custom-call(bf16[8,5120]{1,0:T(8,128)(2,1)} %hid_hbm.1, bf16[8,256,128]{2,1,0:T(8,128)(2,1)} %bitcast.2, bf16[8,256,128]{2,1,0:T(8,128)(2,1)} %bitcast.3, bf16[5120,384]{1,0:T(8,128)(2,1)} %wq_hbm.1, bf16[5120,128]{1,0:T(8,128)(2,1)} %wk_hbm.1, bf16[5120,128]{1,0:T(8,128)(2,1)} %wv_hbm.1, ...), custom_call_target="tpu_custom_call" | custom-call | tf_op jit(solution)/shard_map/pallas_call | solution.py:645
  44.1 1.6 %copy.14 = bf16[2,8,5120]{2,1,0:T(8,128)(2,1)} copy(bf16[2,8,5120]{2,1,0:T(8,128)(2,1)} %shard_map.118) | data formatting | bytes 327680

commit v2 on v1

--- a/solution.py
+++ b/solution.py
@@ -190,19 +190,41 @@
     def _(c):
         out_weight_copy(c).start()
 
+    def far_first(n):
+        odd = lax.rem(n, 2)
+        return tps // 2 + (lax.div(n, 2) + odd) * (1 - 2 * odd)
+
+    sizes = (4, 4, 2) if reps == 32 else (reps,)
+
+    def other_reps(visit):
+        def partner(n):
+            peer, stride = 0, 1
+            for size in reversed(sizes):
+                own = lax.rem(lax.div(r, stride), size)
+                step = lax.rem(lax.div(n, stride), size) + size // 2
+                peer = peer + lax.rem(own + step, size) * stride
+                stride *= size
+            return peer
+
+        own, stride = 0, 1
+        for size in reversed(sizes):
+            own, stride = own + (size - size // 2) * stride, stride * size
+        for low, high in ((0, own), (own + 1, reps)):
+
+            @pl.loop(low, high)
+            def _(n):
+                visit(partner(n))
+
     barrier = pltpu.get_barrier_semaphore()
 
-    @pl.loop(1, reps)
-    def _(d):
-        pl.semaphore_signal(
-            barrier, inc=1, device_id=(lax.rem(r + d, reps), t), device_id_type=MESH
-        )
-
-    @pl.loop(1, tps)
-    def _(d):
-        pl.semaphore_signal(
-            barrier, inc=1, device_id=(r, lax.rem(t + d, tps)), device_id_type=MESH
-        )
+    def greet(to):
+        pl.semaphore_signal(barrier, inc=1, device_id=to, device_id_type=MESH)
+
+    other_reps(lambda peer: greet((peer, t)))
+
+    @pl.loop(0, tps - 1)
+    def _(n):
+        greet((r, lax.rem(t + far_first(n), tps)))
 
     small[1].wait()
     id_send[...] = jnp.zeros_like(id_send)
@@ -210,16 +232,17 @@
     pl.semaphore_wait(barrier, reps + tps - 2)
 
     def to_all_reps(src, dst, send_sem, recv_sem):
-        @pl.loop(1, reps)
-        def _(d):
+        def send(peer):
             pltpu.make_async_remote_copy(
                 src_ref=src,
                 dst_ref=dst.at[r],
                 send_sem=send_sem,
                 recv_sem=recv_sem,
-                device_id=(lax.rem(r + d, reps), t),
+                device_id=(peer, t),
                 device_id_type=MESH,
             ).start()
+
+        other_reps(send)
 
     def wait_reps(dst, sem):
         blocks = dst.at[pl.ds(0, reps - 1)]
@@ -403,10 +426,6 @@
             device_id=(r, to),
             device_id_type=MESH,
         )
-
-    def far_first(n):
-        odd = lax.rem(n, 2)
-        return tps // 2 + (lax.div(n, 2) + odd) * (1 - 2 * odd)
 
     def output_sum(step, attended, wait_weights, meanwhile):
         @pl.loop(0, tps - 1)
@@ -642,16 +661,7 @@
         dma,
         dma((2,)),
     ]
-    return pl.pallas_call(
-        functools.partial(kernel, reps, tps),
-        out_shape=jax.ShapeDtypeStruct((steps, rows, model), BF16),
-        in_specs=[pl.BlockSpec(memory_space=pl.ANY)] * 12,
-        out_specs=pl.BlockSpec(memory_space=pl.ANY),
-        scratch_shapes=scratch,
-        compiler_params=pltpu.CompilerParams(
-            collective_id=0, has_side_effects=True, vmem_limit_bytes=60 * 2**20
-        ),
-    )(
+    operands = [
         hidden_in,
         key_cache.reshape(rows, capacity, head),
         value_cache.reshape(rows, capacity, head),
@@ -664,6 +674,18 @@
         countdown_ids,
         lengths,
         source_slot,
+    ]
+    return pl.pallas_call(
+        functools.partial(kernel, reps, tps),
+        out_shape=jax.ShapeDtypeStruct((steps, rows, model), BF16),
+        in_specs=[pl.BlockSpec(memory_space=pl.ANY)] * 12,
+        out_specs=pl.BlockSpec(memory_space=pl.ANY),
+        scratch_shapes=scratch,
+        compiler_params=pltpu.CompilerParams(
+            collective_id=0, has_side_effects=True, vmem_limit_bytes=48 * 2**20
+        ),
+    )(
+        *[pltpu.with_memory_space_constraint(x, pltpu.HBM) for x in operands]
     )
 
 

time: 45.8 us -> 44.2 us (0.965)
  local copies, waits for them, and re-layouts: 1.59 us -> 0.67 us
  Pallas kernels: 44.1 us -> 43.5 us
    unnamed x1, local copies, waits for them, and re-layouts: 1.59 us -> 0.67 us
    pallas_call x1, Pallas kernels: 44.1 us -> 43.5 us  [body(): pl.pallas_call(functools.partial(kernel, reps, tps), out_shape=jax.ShapeD...]
where the time goes in v2:
time: 44.2 us
  Pallas kernels  43.5 us (98%)
  local copies, waits for them, and re-layouts  0.67 us (2%)
    pallas_call x1, Pallas kernels, body(): pl.pallas_call(functools.partial(kernel, reps, tps), out_shape=jax.ShapeD...  43.5 us

profile of v2, /device:TPU:1, one launch (start us, length us, event | category | flops | bytes accessed | tf_op | source)
XLA Modules:
  0.0 44.2 jit_solution(5065505450295992602)
XLA Ops:
  0.0 43.5 %shard_map.118 = bf16[2,8,5120]{2,1,0:T(8,128)(2,1)S(1)} custom-call(bf16[8,5120]{1,0:T(8,128)(2,1)} %hid_hbm.1, bf16[8,256,128]{2,1,0:T(8,128)(2,1)} %bitcast.2, bf16[8,256,128]{2,1,0:T(8,128)(2,1)} %bitcast.3, bf16[5120,384]{1,0:T(8,128)(2,1)} %wq_hbm.1, bf16[5120,128]{1,0:T(8,128)(2,1)} %wk_hbm.1, bf16[5120,128]{1,0:T(8,128)(2,1)} %wv_hbm.1, ...), custom_call_target="tpu_custom_call" | custom-call | tf_op jit(solution)/shard_map/pallas_call | solution.py:678
  43.5 0.7 %copy.14 = bf16[2,8,5120]{2,1,0:T(8,128)(2,1)} copy(bf16[2,8,5120]{2,1,0:T(8,128)(2,1)S(1)} %shard_map.118) | data formatting | bytes 327680

commit v3 on v2

--- a/solution.py
+++ b/solution.py
@@ -132,6 +132,42 @@
     erows = row_send.shape[0]
     arows = att_send.shape[0]
 
+    def far_first(n):
+        odd = lax.rem(n, 2)
+        return tps // 2 + (lax.div(n, 2) + odd) * (1 - 2 * odd)
+
+    sizes = (4, 4, 2) if reps == 32 else (reps,)
+
+    def other_reps(visit):
+        def partner(n):
+            peer, stride = 0, 1
+            for size in reversed(sizes):
+                own = lax.rem(lax.div(r, stride), size)
+                step = lax.rem(lax.div(n, stride), size) + size // 2
+                peer = peer + lax.rem(own + step, size) * stride
+                stride *= size
+            return peer
+
+        own, stride = 0, 1
+        for size in reversed(sizes):
+            own, stride = own + (size - size // 2) * stride, stride * size
+        for low, high in ((0, own), (own + 1, reps)):
+
+            @pl.loop(low, high)
+            def _(n):
+                visit(partner(n))
+
+    barrier = pltpu.get_barrier_semaphore()
+
+    def greet(to):
+        pl.semaphore_signal(barrier, inc=1, device_id=to, device_id_type=MESH)
+
+    other_reps(lambda peer: greet((peer, t)))
+
+    @pl.loop(0, tps - 1)
+    def _(n):
+        greet((r, lax.rem(t + far_first(n), tps)))
+
     def chunk_cols(c):
         return pl.ds(pl.multiple_of(c * chunk, LANES), chunk)
 
@@ -190,47 +226,6 @@
     def _(c):
         out_weight_copy(c).start()
 
-    def far_first(n):
-        odd = lax.rem(n, 2)
-        return tps // 2 + (lax.div(n, 2) + odd) * (1 - 2 * odd)
-
-    sizes = (4, 4, 2) if reps == 32 else (reps,)
-
-    def other_reps(visit):
-        def partner(n):
-            peer, stride = 0, 1
-            for size in reversed(sizes):
-                own = lax.rem(lax.div(r, stride), size)
-                step = lax.rem(lax.div(n, stride), size) + size // 2
-                peer = peer + lax.rem(own + step, size) * stride
-                stride *= size
-            return peer
-
-        own, stride = 0, 1
-        for size in reversed(sizes):
-            own, stride = own + (size - size // 2) * stride, stride * size
-        for low, high in ((0, own), (own + 1, reps)):
-
-            @pl.loop(low, high)
-            def _(n):
-                visit(partner(n))
-
-    barrier = pltpu.get_barrier_semaphore()
-
-    def greet(to):
-        pl.semaphore_signal(barrier, inc=1, device_id=to, device_id_type=MESH)
-
-    other_reps(lambda peer: greet((peer, t)))
-
-    @pl.loop(0, tps - 1)
-    def _(n):
-        greet((r, lax.rem(t + far_first(n), tps)))
-
-    small[1].wait()
-    id_send[...] = jnp.zeros_like(id_send)
-    id_send[:, 0:rows] = ids_v[...]
-    pl.semaphore_wait(barrier, reps + tps - 2)
-
     def to_all_reps(src, dst, send_sem, recv_sem):
         def send(peer):
             pltpu.make_async_remote_copy(
@@ -247,9 +242,6 @@
     def wait_reps(dst, sem):
         blocks = dst.at[pl.ds(0, reps - 1)]
         pltpu.make_async_copy(blocks, blocks, sem).wait()
-
-    to_all_reps(id_send, id_recv, id_ssem, id_rsem)
-    id_recv[r] = id_send[...]
 
     small[0].wait()
     src0 = src_v[0:1, :].astype(F32)
@@ -322,6 +314,14 @@
         angles = place.astype(F32) * frequency
         return jnp.cos(angles), jnp.sin(angles) * sign
 
+    small[1].wait()
+    id_send[...] = jnp.zeros_like(id_send)
+    id_send[:, 0:rows] = ids_v[...]
+    pl.semaphore_wait(barrier, reps + tps - 2)
+
+    to_all_reps(id_send, id_recv, id_ssem, id_rsem)
+    id_recv[r] = id_send[...]
+
     token_lane = iota((rows, tokens), 1)
 
     def token_pick(ids):
@@ -367,13 +367,14 @@
         return acc * lax.rsqrt(mean + EPSILON)
 
     zero_carry = (jnp.zeros((rows, qcols + 2 * LANES), F32), jnp.zeros((rows, LANES), F32))
-    cap_lane = iota((rows, capacity), 1)
     scale = LANES**-0.5
 
     def round16(x):
         return x.astype(BF16).astype(F32)
 
-    def attend(qkv, place, fresh):
+    def attend(qkv, place, which, fresh):
+        count = qkv.shape[0]
+        cap_lane = iota((count, capacity), 1)
         cosine, sine = turns(place)
 
         def rotate(x):
@@ -384,14 +385,14 @@
         fresh_value = round16(qkv[:, qcols + LANES :])
         fresh = fresh + [(fresh_key, fresh_value, place)]
         stacked = jnp.concatenate(queries, axis=0).astype(BF16)
-        scores = [jnp.zeros((rows, capacity), F32)] * heads
+        scores = [jnp.zeros((count, capacity), F32)] * heads
         for i in range(rows):
             one = lax.dot_general(
                 stacked, keys_v[i], (((1,), (1,)), ((), ())), preferred_element_type=F32
             )
             for h in range(heads):
-                scores[h] = jnp.where(sub8 == i, one[h * rows : (h + 1) * rows], scores[h])
-        weights, extra = [], []
+                scores[h] = jnp.where(which == i, one[h * count : (h + 1) * count], scores[h])
+        weights, extra, totals = [], [], []
         for h in range(heads):
             s = scores[h] * scale
             news = [jnp.sum(queries[h] * k, axis=1, keepdims=True) * scale for k, _, _ in fresh]
@@ -400,22 +401,22 @@
             s = jnp.where(cap_lane <= place, s, -jnp.inf)
             top = jnp.max(s, axis=1, keepdims=True)
             e = jnp.exp(s - top)
-            total = jnp.sum(e, axis=1, keepdims=True)
-            w = e / total
+            totals.append(jnp.sum(e, axis=1, keepdims=True))
             for _, _, at in fresh:
-                w = jnp.where(cap_lane == at, 0.0, w)
-            weights.append(w)
-            extra.append([round16(jnp.exp(new - top) / total) for new in news])
+                e = jnp.where(cap_lane == at, 0.0, e)
+            weights.append(e)
+            extra.append([round16(jnp.exp(new - top)) for new in news])
         stacked = jnp.concatenate(weights, axis=0).astype(BF16)
-        outs = [jnp.zeros((rows, LANES), F32)] * heads
+        outs = [jnp.zeros((count, LANES), F32)] * heads
         for i in range(rows):
             one = dot(stacked, values_v[i])
             for h in range(heads):
-                outs[h] = jnp.where(sub8 == i, one[h * rows : (h + 1) * rows], outs[h])
+                outs[h] = jnp.where(which == i, one[h * count : (h + 1) * count], outs[h])
         for h in range(heads):
             for w, (_, v, _) in zip(extra[h], fresh):
                 outs[h] = outs[h] + w * v
-        return jnp.concatenate(outs, axis=0).astype(BF16), fresh
+            outs[h] = round16(outs[h] / totals[h])
+        return outs, fresh
 
     def part_copy(step, to, src):
         return pltpu.make_async_remote_copy(
@@ -482,41 +483,53 @@
         wide_v[...] += dot((mixture * gain_chunk(c)).astype(BF16), wqkv_v[c])
         sums_v[...] += squares_of(mixture)
 
-    wait_reps(id_recv, id_rsem)
-    id_rows = [jnp.zeros((rows, LANES), F32), jnp.zeros((rows, LANES), F32)]
-    for h in range(reps):
-        block = id_recv[h].astype(F32)
-        for step, slot in enumerate((to0, to1)):
-            id_rows[step] = jnp.where((slot >> 3) == h, block[step : step + 1, :], id_rows[step])
-    ids = []
-    for step, slot in enumerate((to0, to1)):
-        mine = jnp.where(lane8 == (slot & (rows - 1)), id_rows[step], 0.0)
-        ids.append(jnp.sum(mine, axis=1, keepdims=True))
-    now_pick, next_pick = [token_pick(i.astype(jnp.int32)) for i in ids]
-    carry = wide_v[0:rows, :], sums_v[0:rows, :]
-    token_sub = iota((tokens, 1), 0).astype(F32)
-    for k, mover in enumerate(movers):
-        token = jnp.sum(jnp.where(mover, ids[0], 0.0), axis=0, keepdims=True)
-        at = slice(rows + k * tokens, rows + (k + 1) * tokens)
-        carry = tuple(
-            jnp.where(
-                mover,
-                jnp.sum(jnp.where(token_sub == token, wide[at, :], 0.0), axis=0, keepdims=True),
-                kept,
-            )
-            for wide, kept in zip((wide_v, sums_v), carry)
-        )
-    qkv = normalise(carry)
+    def mover_value(mover, column):
+        return jnp.sum(jnp.where(mover, column, 0.0), axis=0, keepdims=True)
+
+    def every_token(column):
+        column = column.astype(F32)
+        blocks = [column]
+        for mover in movers:
+            blocks.append(jnp.broadcast_to(mover_value(mover, column), (tokens, 1)))
+        return jnp.concatenate(blocks, axis=0).astype(jnp.int32)
+
+    wide = normalise((wide_v[...], sums_v[...]))
     for copy in cache_copies:
         copy.wait()
-    attended, fresh = attend(qkv, position, [])
-    attended = spread_groups(attended, rows)
+    outs, fresh = attend(wide, every_token(position), every_token(sub8), [])
+
+    wait_reps(id_recv, id_rsem)
+
+    def slot_tokens(step, slot):
+        found = jnp.zeros((rows, LANES), F32)
+        for h in range(reps):
+            block = id_recv[h, step : step + 1, :].astype(F32)
+            found = jnp.where((slot >> 3) == h, block, found)
+        found = jnp.where(lane8 == (slot & (rows - 1)), found, 0.0)
+        return jnp.sum(found, axis=1, keepdims=True)
+
+    now = slot_tokens(0, to0)
+    token_sub = iota((tokens, 1), 0).astype(F32)
+    takes = [token_sub == mover_value(mover, now) for mover in movers]
+
+    def choose(x):
+        kept = x[0:rows]
+        for k, (mover, take) in enumerate(zip(movers, takes)):
+            block = x[rows + k * tokens : rows + (k + 1) * tokens]
+            kept = jnp.where(mover, mover_value(take, block), kept)
+        return kept
+
+    attended = jnp.concatenate([choose(x) for x in outs], axis=1).astype(BF16)
+    ((fresh_key, fresh_value, _),) = fresh
+    fresh = [(choose(fresh_key), choose(fresh_value), position)]
 
     def find_tokens():
+        next_pick = token_pick(slot_tokens(1, to1).astype(jnp.int32))
         picks = jnp.concatenate([next_pick, slot_pick], axis=0).astype(BF16)
         for c in range(tps):
             tab_v[c] = dot(picks, table_v[c])
-        mix.append(hidden_chunk(t) + dot(now_pick.astype(BF16), table_v[t]))
+        now_pick = token_pick(now.astype(jnp.int32)).astype(BF16)
+        mix.append(hidden_chunk(t) + dot(now_pick, table_v[t]))
 
     mix = []
     summed = output_sum(0, attended, True, find_tokens)
@@ -536,7 +549,8 @@
 
     qkv = normalise(lax.fori_loop(0, tps - 1, next_project, carry))
 
-    attended, _ = attend(qkv, position + 1, fresh)
+    outs, _ = attend(qkv, position + 1, sub8, fresh)
+    attended = jnp.concatenate(outs, axis=0).astype(BF16)
     att_send[...] = dot(att_pick, attended).astype(BF16)
     to_all_reps(att_send, att_recv, att_ssem, att_rsem)
     att_recv[r] = att_send[...]
@@ -565,11 +579,11 @@
         copy.start()
         return copy
 
-    outs = []
-    summed = output_sum(1, attended, False, lambda: outs.append(result(1, first_buf, first_v)))
+    results = []
+    summed = output_sum(1, attended, False, lambda: results.append(result(1, first_buf, first_v)))
     hidden = last + summed
     gather_start(2, last_buf, pack(hidden))
-    outs.append(result(2, last_buf, last_v))
+    results.append(result(2, last_buf, last_v))
 
     wait_reps(id_recv, id_ssem)
     wait_reps(row_recv, row_ssem)
@@ -583,7 +597,7 @@
         for which, buf in enumerate((home_buf, first_buf, last_buf)):
             gather_copy(which, buf, to, t).wait_send()
 
-    for copy in outs:
+    for copy in results:
         copy.wait()
 
 

time: 44.2 us -> 43.9 us (level)
  no operation moved by 1% of the time
where the time goes in v3:
time: 43.9 us; the launch traced here: 43.8 us
  Pallas kernels  43.2 us (98%)
  local copies, waits for them, and re-layouts  0.67 us (2%)
    pallas_call x1, Pallas kernels, body(): pl.pallas_call(functools.partial(kernel, reps, tps), out_shape=jax.ShapeD...  43.2 us

profile of v3, /device:TPU:1, one launch (start us, length us, event | category | flops | bytes accessed | tf_op | source)
XLA Modules:
  0.0 43.8 jit_solution(12916186946850756620)
XLA Ops:
  0.0 43.2 %shard_map.118 = bf16[2,8,5120]{2,1,0:T(8,128)(2,1)S(1)} custom-call(bf16[8,5120]{1,0:T(8,128)(2,1)} %hid_hbm.1, bf16[8,256,128]{2,1,0:T(8,128)(2,1)} %bitcast.2, bf16[8,256,128]{2,1,0:T(8,128)(2,1)} %bitcast.3, bf16[5120,384]{1,0:T(8,128)(2,1)} %wq_hbm.1, bf16[5120,128]{1,0:T(8,128)(2,1)} %wk_hbm.1, bf16[5120,128]{1,0:T(8,128)(2,1)} %wv_hbm.1, ...), custom_call_target="tpu_custom_call" | custom-call | tf_op jit(solution)/shard_map/pallas_call | solution.py:692
  43.2 0.7 %copy.14 = bf16[2,8,5120]{2,1,0:T(8,128)(2,1)} copy(bf16[2,8,5120]{2,1,0:T(8,128)(2,1)S(1)} %shard_map.118) | data formatting | bytes 327680

commit v4 on v3

--- a/solution.py
+++ b/solution.py
@@ -73,7 +73,7 @@
     ids_hbm,
     len_hbm,
     src_hbm,
-    out_hbm,
+    out_ref,
     hid_v,
     keys_v,
     values_v,
@@ -89,8 +89,6 @@
     sums_v,
     tab_v,
     rank_v,
-    first_v,
-    last_v,
     id_send,
     id_recv,
     part_send,
@@ -103,6 +101,7 @@
     att_send,
     att_recv,
     load_sem,
+    cache_sem,
     weight_sem,
     out_w_sem,
     id_ssem,
@@ -115,7 +114,6 @@
     row_rsem,
     att_ssem,
     att_rsem,
-    out_sem,
 ):
     r = lax.axis_index("rep")
     t = lax.axis_index("tp")
@@ -213,8 +211,11 @@
             copy.start()
 
     cache_copies = [
-        pltpu.make_async_copy(keys_hbm, keys_v, load_sem.at[5]),
-        pltpu.make_async_copy(values_hbm, values_v, load_sem.at[6]),
+        pltpu.make_async_copy(
+            hbm.at[i], vmem.at[i // 2, :, pl.ds(i % 2 * LANES, LANES)], cache_sem.at[which, i]
+        )
+        for which, (hbm, vmem) in enumerate(((keys_hbm, keys_v), (values_hbm, values_v)))
+        for i in range(rows)
     ]
     for copy in cache_copies:
         copy.start()
@@ -386,12 +387,24 @@
         fresh = fresh + [(fresh_key, fresh_value, place)]
         stacked = jnp.concatenate(queries, axis=0).astype(BF16)
         scores = [jnp.zeros((count, capacity), F32)] * heads
-        for i in range(rows):
-            one = lax.dot_general(
-                stacked, keys_v[i], (((1,), (1,)), ((), ())), preferred_element_type=F32
+        none = jnp.zeros_like(stacked)
+        sides = jnp.concatenate(
+            [
+                jnp.concatenate([stacked, none], axis=1),
+                jnp.concatenate([none, stacked], axis=1),
+            ],
+            axis=0,
+        )
+        for pair in range(rows // 2):
+            both = lax.dot_general(
+                sides, keys_v[pair], (((1,), (1,)), ((), ())), preferred_element_type=F32
             )
-            for h in range(heads):
-                scores[h] = jnp.where(which == i, one[h * count : (h + 1) * count], scores[h])
+            for side in range(2):
+                for h in range(heads):
+                    at = (side * heads + h) * count
+                    scores[h] = jnp.where(
+                        which == 2 * pair + side, both[at : at + count], scores[h]
+                    )
         weights, extra, totals = [], [], []
         for h in range(heads):
             s = scores[h] * scale
@@ -408,10 +421,14 @@
             extra.append([round16(jnp.exp(new - top)) for new in news])
         stacked = jnp.concatenate(weights, axis=0).astype(BF16)
         outs = [jnp.zeros((count, LANES), F32)] * heads
-        for i in range(rows):
-            one = dot(stacked, values_v[i])
-            for h in range(heads):
-                outs[h] = jnp.where(which == i, one[h * count : (h + 1) * count], outs[h])
+        for pair in range(rows // 2):
+            both = dot(stacked, values_v[pair])
+            for side in range(2):
+                one = both[:, side * LANES : (side + 1) * LANES]
+                for h in range(heads):
+                    outs[h] = jnp.where(
+                        which == 2 * pair + side, one[h * count : (h + 1) * count], outs[h]
+                    )
         for h in range(heads):
             for w, (_, v, _) in zip(extra[h], fresh):
                 outs[h] = outs[h] + w * v
@@ -567,23 +584,19 @@
     attended = (dot(att_far, received) + dot(att_near, attended)).astype(BF16)
     attended = spread_groups(attended, rows)
 
-    def result(which, buf, out_v):
+    def result(which, buf):
         @pl.loop(1, tps)
         def _(d):
             gather_copy(which, buf, t, lax.rem(t + d, tps)).wait_recv()
 
         for c in range(tps):
             cols = slice(c * chunk, (c + 1) * chunk)
-            out_v[:, cols] = unpack(buf[c], chunk).astype(BF16)
-        copy = pltpu.make_async_copy(out_v, out_hbm.at[which - 1], out_sem.at[which - 1])
-        copy.start()
-        return copy
-
-    results = []
-    summed = output_sum(1, attended, False, lambda: results.append(result(1, first_buf, first_v)))
+            out_ref[which - 1, :, cols] = unpack(buf[c], chunk).astype(BF16)
+
+    summed = output_sum(1, attended, False, lambda: result(1, first_buf))
     hidden = last + summed
     gather_start(2, last_buf, pack(hidden))
-    results.append(result(2, last_buf, last_v))
+    result(2, last_buf)
 
     wait_reps(id_recv, id_ssem)
     wait_reps(row_recv, row_ssem)
@@ -596,9 +609,6 @@
             part_copy(step, to, t).wait_send()
         for which, buf in enumerate((home_buf, first_buf, last_buf)):
             gather_copy(which, buf, to, t).wait_send()
-
-    for copy in results:
-        copy.wait()
 
 
 def body(
@@ -633,8 +643,8 @@
     dma, vmem = pltpu.SemaphoreType.DMA, pltpu.VMEM
     scratch = [
         vmem((rows, model), BF16),
-        vmem((rows, capacity, head), BF16),
-        vmem((rows, capacity, head), BF16),
+        vmem((rows // 2, capacity, 2 * head), BF16),
+        vmem((rows // 2, capacity, 2 * head), BF16),
         vmem((tps, chunk, qcols + 2 * head), BF16),
         vmem((tps, qcols, chunk), BF16),
         vmem((model,), BF16),
@@ -647,8 +657,6 @@
         vmem((rows + MOVE * tokens, LANES), F32),
         vmem((tps, 2 * rows, chunk), F32),
         vmem((total_rows, LANES), F32),
-        vmem((rows, model), BF16),
-        vmem((rows, model), BF16),
         vmem((steps, LANES), jnp.int32),
         vmem((reps, steps, LANES), jnp.int32),
         vmem((steps, tps) + block, BF16),
@@ -661,6 +669,7 @@
         vmem((arows, LANES), BF16),
         vmem((reps, arows, LANES), BF16),
         dma((7 + tps,)),
+        dma((2, rows)),
         dma((3, tps)),
         dma((tps,)),
         dma,
@@ -673,7 +682,6 @@
         dma,
         dma,
         dma,
-        dma((2,)),
     ]
     operands = [
         hidden_in,
@@ -691,9 +699,9 @@
     ]
     return pl.pallas_call(
         functools.partial(kernel, reps, tps),
-        out_shape=jax.ShapeDtypeStruct((steps, rows, model), BF16),
+        out_shape=pltpu.VMEM((steps, rows, model), BF16),
         in_specs=[pl.BlockSpec(memory_space=pl.ANY)] * 12,
-        out_specs=pl.BlockSpec(memory_space=pl.ANY),
+        out_specs=pl.BlockSpec(memory_space=pltpu.VMEM),
         scratch_shapes=scratch,
         compiler_params=pltpu.CompilerParams(
             collective_id=0, has_side_effects=True, vmem_limit_bytes=48 * 2**20

time: 43.9 us -> 42.8 us (0.975)
  Pallas kernels: 43.2 us -> 42 us
    pallas_call x1, Pallas kernels: 43.2 us -> 42 us  [body(): pl.pallas_call(functools.partial(kernel, reps, tps), out_shape=pltpu.VMEM...]
where the time goes in v4:
time: 42.8 us; the launch traced here: 42.7 us
  Pallas kernels  42 us (98%)
  local copies, waits for them, and re-layouts  0.67 us (2%)
    pallas_call x1, Pallas kernels, body(): pl.pallas_call(functools.partial(kernel, reps, tps), out_shape=pltpu.VMEM...  42 us

profile of v4, /device:TPU:1, one launch (start us, length us, event | category | flops | bytes accessed | tf_op | source)
XLA Modules:
  0.0 42.7 jit_solution(6479152156275851000)
XLA Ops:
  0.0 42.0 %shard_map.118 = bf16[2,8,5120]{2,1,0:T(8,128)(2,1)S(1)} custom-call(bf16[8,5120]{1,0:T(8,128)(2,1)} %hid_hbm.1, bf16[8,256,128]{2,1,0:T(8,128)(2,1)} %bitcast.2, bf16[8,256,128]{2,1,0:T(8,128)(2,1)} %bitcast.3, bf16[5120,384]{1,0:T(8,128)(2,1)} %wq_hbm.1, bf16[5120,128]{1,0:T(8,128)(2,1)} %wk_hbm.1, bf16[5120,128]{1,0:T(8,128)(2,1)} %wv_hbm.1, ...), custom_call_target="tpu_custom_call" | custom-call | tf_op jit(solution)/shard_map/pallas_call | solution.py:700
  42.0 0.7 %copy.14 = bf16[2,8,5120]{2,1,0:T(8,128)(2,1)} copy(bf16[2,8,5120]{2,1,0:T(8,128)(2,1)S(1)} %shard_map.118) | data formatting | bytes 327680
